TPU v7x, 32 devices: a whole 2x2x4 slice. The times are simulated.
32 devices in a mesh: cell: 8 (over y, x, core), state: 4 (over z).
Axes of the slice: x: 2, y: 2, z: 4, core: 2. Of those that a mesh axis runs over, the one named last changes fastest.
Arguments:
- start_block: float32 [1024, 4096], P('state', 'cell'), may hold values from -6 to 6
- connectivity: int32 [16, 343], P('cell'), may hold values from 0 to 575, as said below
- cell_matrices: bfloat16 [16, 343, 343], P('cell'), may hold values from -4 to 4
- bounds: float32 [3], replicated, may hold values from -1 to 32, as said below
Outputs:
- filtered: float32 [1024, 4096], P('state', 'cell')
- projected: float32 [1024, 1024], P('cell', 'state')
Inputs may be any that keep to these rules, and one draw needn't show every extreme that they name: `connectivity`: each row names 343 different local nodes; numbers below 512 are nodes owned by the index of cell that holds the cell, the others the first 64 nodes of the next index of cell, cyclically. `bounds`: lowest < cut < upper, and every eigenvalue of H lies above lowest.
All inputs are finite; a program needn't handle non-finite values.
Results may differ from a plain program's by a relative error of at most 0.0016.
Values may be sent and summed in bfloat16 or wider, within the bound.
A program may use at most 64 MiB of HBM per device.

v0:
```python
import functools

import jax
import jax.numpy as jnp
from jax import lax
from jax.experimental import pallas as pl
from jax.experimental.pallas import tpu as pltpu
from jax.sharding import PartitionSpec as P

DEGREE = 8
MESH = pl.DeviceIdType.MESH


def matmul(left, right):
    return jnp.dot(left, right, preferred_element_type=jnp.float32)


def filter_kernel(
    count, start, links, cells, bounds, filtered, low, image,
    matrix, stack, field, before, inner, outgoing, incoming, ghost, sends, receives, ghost_sems,
):
    states, owned = start.shape
    shared = owned // 8
    both = 2 * shared
    extent = owned + shared
    rest = extent - both
    first = 2 * both
    second = first + (rest + 127) // 128 * 128
    me = lax.axis_index("cell")
    right, left = lax.rem(me + 1, count), lax.rem(me + count - 1, count)

    barrier = pltpu.get_barrier_semaphore()
    for neighbour in (left, right):
        pl.semaphore_signal(barrier, inc=1, device_id={"cell": neighbour}, device_id_type=MESH)

    field[0:both, :] = start[:, 0:both].T
    stack[0:both, :] = field[0:both, :].astype(jnp.bfloat16)
    pl.semaphore_wait(barrier, 2)
    ghost_copy = pltpu.make_async_remote_copy(
        src_ref=outgoing.at[pl.ds(0, shared)],
        dst_ref=ghost,
        send_sem=ghost_sems.at[0],
        recv_sem=ghost_sems.at[1],
        device_id={"cell": left},
        device_id_type=MESH,
    )
    outgoing[0:shared, :] = field[0:shared, :]
    ghost_copy.start()

    whole = start[...].T
    field[both:, :] = whole[shared:, :]
    before[...] = jnp.zeros_like(before)

    for cell in range(links.shape[0]):
        link = links[cell : cell + 1, :]
        row = jnp.where(
            link < shared, link, jnp.where(link < owned, link + shared, link - (owned - shared))
        )
        spread = lax.broadcasted_iota(jnp.int32, (extent, links.shape[1]), 0) == row
        spread = jnp.where(spread, 1.0, 0.0).astype(jnp.bfloat16)
        half_way = matmul(spread, cells[cell]).astype(jnp.bfloat16)
        placed = lax.dot_general(
            half_way, spread, (((1,), (1,)), ((), ())), preferred_element_type=jnp.float32
        ).astype(jnp.bfloat16)
        matrix[:, cell * both : (cell + 1) * both] = placed[:, 0:both]
        begin = first if cell == 0 else second
        matrix[:, begin : begin + rest] = placed[:, both:]
    if second > first + rest:
        matrix[:, first + rest : second] = jnp.zeros((extent, second - first - rest), jnp.bfloat16)
        stack[first + rest : second, :] = jnp.zeros((second - first - rest, states), jnp.bfloat16)

    def put_rest():
        rounded = field[both:, :].astype(jnp.bfloat16)
        stack[first : first + rest, :] = rounded
        stack[second : second + rest, :] = rounded
        inner[...] = matmul(matrix[0:both, first:], stack[first:, :])

    def put_shared():
        rounded = field[0:both, :].astype(jnp.bfloat16)
        stack[0:both, :] = rounded
        stack[both:first, :] = rounded
        outgoing[...] = inner[...] + matmul(matrix[0:both, 0:first], stack[0:first, :])

    def copies(slot):
        to_left = pltpu.make_async_remote_copy(
            src_ref=outgoing.at[pl.ds(0, shared)],
            dst_ref=incoming.at[slot, pl.ds(shared, shared)],
            send_sem=sends.at[0],
            recv_sem=receives.at[slot, 0],
            device_id={"cell": left},
            device_id_type=MESH,
        )
        to_right = pltpu.make_async_remote_copy(
            src_ref=outgoing.at[pl.ds(shared, shared)],
            dst_ref=incoming.at[slot, pl.ds(0, shared)],
            send_sem=sends.at[1],
            recv_sem=receives.at[slot, 1],
            device_id={"cell": right},
            device_id_type=MESH,
        )
        return to_left, to_right

    put_rest()
    ghost_copy.wait()
    field[shared:both, :] = ghost[...]
    put_shared()
    for copy in copies(0):
        copy.start()

    def vector(value):
        return jnp.full((1, states), value, jnp.float32)

    lowest, cut, upper = vector(bounds[0]), vector(bounds[1]), vector(bounds[2])
    half = (upper - cut) / 2.0
    centre = (upper + cut) / 2.0
    sigma_first = half / (lowest - centre)
    tau = 2.0 / sigma_first

    def degree_step(step, carry):
        alpha, beta, sigma = carry
        slot = lax.rem(step, 2)
        new_rest = (
            matmul(matrix[both:, :], stack[...]) - centre * field[both:, :]
        ) * alpha - beta * before[both:, :]
        before[both:, :] = field[both:, :]
        field[both:, :] = new_rest
        put_rest()
        for copy in copies(slot):
            copy.wait()
        new_shared = (
            outgoing[...] + incoming[slot] - centre * field[0:both, :]
        ) * alpha - beta * before[0:both, :]
        before[0:both, :] = field[0:both, :]
        field[0:both, :] = new_shared
        put_shared()
        for copy in copies(lax.rem(step + 1, 2)):
            copy.start()
        sigma_new = 1.0 / (tau - sigma)
        return 2.0 * sigma_new / half, sigma * sigma_new, sigma_new

    lax.fori_loop(
        0, DEGREE, degree_step, (sigma_first / half, jnp.zeros_like(half), sigma_first)
    )

    result = jnp.concatenate([field[0:shared, :], field[both:, :]], axis=0).T
    filtered[...] = result
    low[...] = result.astype(jnp.bfloat16)
    image[shared:, :] = matmul(matrix[both:, :], stack[...]).astype(jnp.bfloat16)
    last = DEGREE % 2
    for copy in copies(last):
        copy.wait()
    image[0:shared, :] = (outgoing[0:shared, :] + incoming[last, 0:shared, :]).astype(jnp.bfloat16)


def filtered_block(start, links, cells, bounds, count):
    states, owned = start.shape
    shared = owned // 8
    both = 2 * shared
    extent = owned + shared
    rest = extent - both
    depth = 2 * both + (rest + 127) // 128 * 128 + rest
    vmem = pl.BlockSpec(memory_space=pltpu.VMEM)
    return pl.pallas_call(
        functools.partial(filter_kernel, count),
        out_shape=(
            jax.ShapeDtypeStruct((states, owned), jnp.float32),
            jax.ShapeDtypeStruct((states, owned), jnp.bfloat16),
            jax.ShapeDtypeStruct((owned, states), jnp.bfloat16),
        ),
        in_specs=[vmem, vmem, vmem, pl.BlockSpec(memory_space=pltpu.SMEM)],
        out_specs=(vmem, vmem, vmem),
        scratch_shapes=[
            pltpu.VMEM((extent, depth), jnp.bfloat16),
            pltpu.VMEM((depth, states), jnp.bfloat16),
            pltpu.VMEM((extent, states), jnp.float32),
            pltpu.VMEM((extent, states), jnp.float32),
            pltpu.VMEM((both, states), jnp.float32),
            pltpu.VMEM((both, states), jnp.float32),
            pltpu.VMEM((2, both, states), jnp.float32),
            pltpu.VMEM((shared, states), jnp.float32),
            pltpu.SemaphoreType.DMA((2,)),
            pltpu.SemaphoreType.DMA((2, 2)),
            pltpu.SemaphoreType.DMA((2,)),
        ],
        compiler_params=pltpu.CompilerParams(
            collective_id=0, has_side_effects=True, vmem_limit_bytes=40 * 1024 * 1024
        ),
    )(start, links, cells, bounds)


def per_device(start_block, connectivity, cell_matrices, bounds, count):
    filtered, low, image = filtered_block(
        start_block, connectivity, cell_matrices, bounds, count
    )
    all_low = lax.all_gather(low, "state", axis=0, tiled=True)
    partial_value = matmul(all_low, image)
    projected = lax.psum_scatter(partial_value, "cell", scatter_dimension=0, tiled=True)
    return (filtered, projected)


def solution(mesh):
    in_specs = (P("state", "cell"), P("cell", None), P("cell", None, None), P())
    out_specs = (P("state", "cell"), P("cell", "state"))
    return jax.shard_map(
        functools.partial(per_device, count=mesh.shape["cell"]),
        mesh=mesh, in_specs=in_specs, out_specs=out_specs, check_vma=False,
    )
```

profile of v0, /device:TPU:0, one launch (start us, length us, event | category | flops | bytes accessed | tf_op | source)
XLA Modules:
  0.0 122.6 jit_solution(3392674874368986031)
XLA Ops:
  7.2 0.0 copy-start.2
  7.2 0.0 copy-start.1
  7.2 0.0 copy-start
  7.2 0.0 all-gather.2.cloned.1.call-start
  7.2 1.2 copy.6.cells
  8.4 0.0 copy-done.2
  8.4 0.0 copy-done.1
  8.4 0.0 copy-done
  8.4 39.2 %shard_map.59 = (f32[256,512]{1,0:T(8,128)S(1)}, bf16[256,512]{1,0:T(8,128)(2,1)}, bf16[512,256]{1,0:T(8,128)(2,1)S(1)}) custom-call(f32[256,512]{1,0:T(8,128)S(1)} %copy-done, s32[2,343]{1,0:T(2,128)S(1)} %copy-done.1, bf16[2,343,343]{2,1,0:T(8,128)(2,1)S(1)} %copy.6.cells, f32[3]{0:T(128)S(1)} %copy-done.2), custom_call_target="tpu_custom_call" | custom-call | tf_op jit(solution)/shard_map/pallas_call | solution.py:163
  47.6 0.0 all-gather.2.cloned.1.call-update
  47.7 0.0 reduce-scatter.2.cloned.1.call-start
  47.7 28.0 %all-gather.2.cloned.1.call-done = bf16[1024,512]{1,0:T(8,128)(2,1)} async-done(((bf16[256,512]{1,0:T(8,128)(2,1)}), bf16[1024,512]{1,0:T(8,128)(2,1)}) %all-gather.2.cloned.1.call-update) | async-done | bytes 1048592 | tf_op jit(solution)/shard_map/all_gather | solution.py:195
  75.7 2.7 %fusion = f32[1024,256]{1,0:T(8,128)} fusion(bf16[1024,512]{1,0:T(8,128)(2,1)} %all-gather.2.cloned.1.call-done, bf16[512,256]{1,0:T(8,128)(2,1)S(1)} %get-tuple-element.7), kind=kOutput, calls=%fused_computation | convolution fusion | flops 268435456 | bytes 2359296 | tf_op jit(solution)/shard_map/dot_general | solution.py:15
  78.4 0.0 reduce-scatter.2.cloned.1.call-update
  78.4 36.6 %reduce-scatter.2.cloned.1.call-done = f32[128,256]{1,0:T(8,128)} async-done(((f32[1024,256]{1,0:T(8,128)}), f32[128,256]{1,0:T(8,128)}) %reduce-scatter.2.cloned.1.call-update) | async-done | bytes 131088 | tf_op jit(solution)/shard_map/reduce_scatter | solution.py:197
  115.0 0.8 copy.8
Async XLA Ops:
  7.2 1.2 %copy-start.2 = (f32[3]{0:T(128)S(1)}, f32[3]{0:T(128)}, u32[]{:S(2)}) copy-start(f32[3]{0:T(128)} %bounds.1) | copy-start | bytes 40
  7.2 1.2 %copy-start.1 = (s32[2,343]{1,0:T(2,128)S(1)}, s32[2,343]{1,0:T(2,128)}, u32[]{:S(2)}) copy-start(s32[2,343]{1,0:T(2,128)} %links.1) | copy-start | bytes 8236
  7.2 1.2 %copy-start = (f32[256,512]{1,0:T(8,128)S(1)}, f32[256,512]{1,0:T(8,128)}, u32[]{:S(2)}) copy-start(f32[256,512]{1,0:T(8,128)} %start.1) | copy-start | bytes 1572868
  7.2 68.5 %all-gather.2.cloned.1.call-start = ((), (), s32[]{:S(2)}) async-start(), calls=%async_computation.1 | async-start | bytes 1310720 | tf_op jit(solution)/shard_map/all_gather | solution.py:195
  47.7 67.3 %reduce-scatter.2.cloned.1.call-start = ((), (), s32[]{:S(2)}) async-start(), calls=%async_computation.2 | async-start | bytes 1179648 | tf_op jit(solution)/shard_map/reduce_scatter | solution.py:197
Sparse Core Ops, SparseCore 0:
  47.8 27.8 all-gather.1
  79.4 35.5 reduce-scatter.1
where the time goes:
time: 123 us
  waiting for transfers between devices  64.6 us (53%)
  Pallas kernels  39.2 us (32%)
  between operations  14.1 us (11%)
  matrix products  2.69 us (2%)
  local copies, waits for them, and re-layouts  1.97 us (2%)
    pallas_call x1, Pallas kernels, filtered_block(): pl.pallas_call(functools.partial(filter_kernel, count), out_shape=(jax.Sh...  39.2 us
    reduce_scatter x1, waiting for transfers between devices, per_device(): lax.psum_scatter(partial_value, 'cell', scatter_dimension=0, tiled=True)  36.6 us
    all_gather x1, waiting for transfers between devices, per_device(): all_low = lax.all_gather(low, 'state', axis=0, tiled=True)  28 us
    dot_general x1, matrix products, matmul(): return jnp.dot(left, right, preferred_element_type=jnp.float32)  2.69 us
  transfers between devices with their start and end apart: 2, of which 2 were waited for; matrix products, arithmetic and copies ran while one was open for 0% of the time, Pallas kernels for 0%

commit v1 on v0

--- a/solution.py
+++ b/solution.py
@@ -16,8 +16,11 @@
 
 
 def filter_kernel(
-    count, start, links, cells, bounds, filtered, low, image,
-    matrix, stack, field, before, inner, outgoing, incoming, ghost, sends, receives, ghost_sems,
+    count, groups, start, links, cells, bounds, filtered, projected,
+    matrix, stack, field, before, inner, outgoing, rounded_out, incoming, ghost,
+    image, lows, parts, swapped, ship, gathered, mine,
+    sends, receives, ghost_sems, along_send, along_recv, swap_send, swap_recv,
+    ship_send, ship_recv,
 ):
     states, owned = start.shape
     shared = owned // 8
@@ -29,13 +32,37 @@
     me = lax.axis_index("cell")
     right, left = lax.rem(me + 1, count), lax.rem(me + count - 1, count)
 
+    rows = projected.shape[0]
+    owners = states // rows
+    chips = count // 2
+    chip, core = me // 2, lax.rem(me, 2)
+    place = lax.axis_index("state")
+
     barrier = pltpu.get_barrier_semaphore()
-    for neighbour in (left, right):
-        pl.semaphore_signal(barrier, inc=1, device_id={"cell": neighbour}, device_id_type=MESH)
+
+    def greet(target):
+        pl.semaphore_signal(barrier, inc=1, device_id=target, device_id_type=MESH)
+
+    greet({"cell": left})
+    greet({"cell": right})
+    for other in range(chips):
+
+        @pl.when(other != chip)
+        def _():
+            greet({"cell": 2 * other + core})
+
+    @pl.when(place > 0)
+    def _():
+        greet({"state": place - 1})
+
+    @pl.when(place < groups - 1)
+    def _():
+        greet({"state": place + 1})
 
     field[0:both, :] = start[:, 0:both].T
     stack[0:both, :] = field[0:both, :].astype(jnp.bfloat16)
-    pl.semaphore_wait(barrier, 2)
+    beside = jnp.minimum(place, 1) + jnp.minimum(groups - 1 - place, 1)
+    pl.semaphore_wait(barrier, 1 + chips + beside)
     ghost_copy = pltpu.make_async_remote_copy(
         src_ref=outgoing.at[pl.ds(0, shared)],
         dst_ref=ghost,
@@ -79,11 +106,13 @@
         rounded = field[0:both, :].astype(jnp.bfloat16)
         stack[0:both, :] = rounded
         stack[both:first, :] = rounded
-        outgoing[...] = inner[...] + matmul(matrix[0:both, 0:first], stack[0:first, :])
+        total = inner[...] + matmul(matrix[0:both, 0:first], stack[0:first, :])
+        outgoing[...] = total
+        rounded_out[...] = total.astype(jnp.bfloat16)
 
     def copies(slot):
         to_left = pltpu.make_async_remote_copy(
-            src_ref=outgoing.at[pl.ds(0, shared)],
+            src_ref=rounded_out.at[pl.ds(0, shared)],
             dst_ref=incoming.at[slot, pl.ds(shared, shared)],
             send_sem=sends.at[0],
             recv_sem=receives.at[slot, 0],
@@ -91,7 +120,7 @@
             device_id_type=MESH,
         )
         to_right = pltpu.make_async_remote_copy(
-            src_ref=outgoing.at[pl.ds(shared, shared)],
+            src_ref=rounded_out.at[pl.ds(shared, shared)],
             dst_ref=incoming.at[slot, pl.ds(0, shared)],
             send_sem=sends.at[1],
             recv_sem=receives.at[slot, 1],
@@ -144,31 +173,173 @@
 
     result = jnp.concatenate([field[0:shared, :], field[both:, :]], axis=0).T
     filtered[...] = result
-    low[...] = result.astype(jnp.bfloat16)
+    lows[place] = result.astype(jnp.bfloat16)
+
+    def hand_on(way, hop):
+        step = 1 - 2 * way
+        block = lax.rem(place - step * hop + groups, groups)
+        return pltpu.make_async_remote_copy(
+            src_ref=lows.at[block],
+            dst_ref=lows.at[block],
+            send_sem=along_send.at[way, hop],
+            recv_sem=along_recv.at[way, hop],
+            device_id={"state": lax.rem(place + step + groups, groups)},
+            device_id_type=MESH,
+        )
+
+    def sends_at(way, hop):
+        if way == 0:
+            return jnp.logical_and(place < groups - 1, place >= hop)
+        return jnp.logical_and(place > 0, place + hop < groups)
+
+    def receives_at(way, hop):
+        if way == 0:
+            return place >= hop + 1
+        return place + hop + 1 < groups
+
+    def block_at(way, hop):
+        return lax.rem(place - (1 - 2 * way) * (hop + 1) + groups, groups)
+
+    def arrival(way, hop):
+        step = 1 - 2 * way
+        block = block_at(way, hop)
+        return pltpu.make_async_remote_copy(
+            src_ref=lows.at[block],
+            dst_ref=lows.at[block],
+            send_sem=along_send.at[way, hop],
+            recv_sem=along_recv.at[way, hop],
+            device_id={"state": lax.rem(place + step + groups, groups)},
+            device_id_type=MESH,
+        )
+
+    for way in range(2):
+
+        @pl.when(sends_at(way, 0))
+        def _():
+            hand_on(way, 0).start()
+
     image[shared:, :] = matmul(matrix[both:, :], stack[...]).astype(jnp.bfloat16)
     last = DEGREE % 2
     for copy in copies(last):
         copy.wait()
     image[0:shared, :] = (outgoing[0:shared, :] + incoming[last, 0:shared, :]).astype(jnp.bfloat16)
 
-
-def filtered_block(start, links, cells, bounds, count):
+    def swap(block, pair):
+        return pltpu.make_async_remote_copy(
+            src_ref=parts.at[block, pl.ds((2 * pair + 1 - core) * rows, rows)],
+            dst_ref=swapped.at[block, pl.ds(pair * rows, rows)],
+            send_sem=swap_send.at[block, pair],
+            recv_sem=swap_recv.at[block, pair],
+            device_id={"cell": chip * 2 + 1 - core},
+            device_id_type=MESH,
+        )
+
+    def owner_of(block, pair):
+        return block * (owners // 2) + pair
+
+    def shipping(block, pair):
+        return pltpu.make_async_remote_copy(
+            src_ref=ship.at[block, pl.ds(pair * rows, rows)],
+            dst_ref=gathered.at[chip],
+            send_sem=ship_send.at[block, pair],
+            recv_sem=ship_recv.at[chip],
+            device_id={"cell": 2 * owner_of(block, pair) + core},
+            device_id_type=MESH,
+        )
+
+    def multiply(block):
+        parts[block] = matmul(lows[block], image[...])
+        for pair in range(owners // 2):
+            swap(block, pair).start()
+
+    def pass_to_owners(block):
+        for pair in range(owners // 2):
+            swap(block, pair).wait()
+            kept = pl.ds(pl.multiple_of((2 * pair + core) * rows, rows), rows)
+            total = parts[block, kept, :] + swapped[block, pair * rows : (pair + 1) * rows, :]
+
+            @pl.when(owner_of(block, pair) == chip)
+            def _():
+                mine[...] = total
+
+            @pl.when(owner_of(block, pair) != chip)
+            def _():
+                ship[block, pair * rows : (pair + 1) * rows, :] = total.astype(jnp.bfloat16)
+                shipping(block, pair).start()
+
+    multiply(place)
+    pass_to_owners(place)
+    for hop in range(groups - 1):
+        for way in range(2):
+
+            @pl.when(receives_at(way, hop))
+            def _():
+                arrival(way, hop).wait_recv()
+                if hop + 1 < groups - 1:
+
+                    @pl.when(sends_at(way, hop + 1))
+                    def _():
+                        hand_on(way, hop + 1).start()
+
+                multiply(block_at(way, hop))
+
+        for way in range(2):
+
+            @pl.when(receives_at(way, hop))
+            def _():
+                pass_to_owners(block_at(way, hop))
+
+    for way in range(2):
+        for hop in range(groups - 1):
+
+            @pl.when(sends_at(way, hop))
+            def _():
+                hand_on(way, hop).wait_send()
+
+    for block in range(groups):
+        for pair in range(owners // 2):
+
+            @pl.when(owner_of(block, pair) != chip)
+            def _():
+                shipping(block, pair).wait_send()
+
+    for other in range(chips):
+
+        @pl.when(other != chip)
+        def _():
+            pltpu.make_async_remote_copy(
+                src_ref=gathered.at[other],
+                dst_ref=gathered.at[other],
+                send_sem=ship_send.at[0, 0],
+                recv_sem=ship_recv.at[other],
+                device_id={"cell": 2 * other + core},
+                device_id_type=MESH,
+            ).wait_recv()
+            mine[...] += gathered[other].astype(jnp.float32)
+
+    projected[...] = mine[...]
+
+
+def filtered_block(start, links, cells, bounds, count, groups):
     states, owned = start.shape
     shared = owned // 8
     both = 2 * shared
     extent = owned + shared
     rest = extent - both
     depth = 2 * both + (rest + 127) // 128 * 128 + rest
+    rows = states * groups // count
+    pairs = states // rows // 2
+    chips = count // 2
     vmem = pl.BlockSpec(memory_space=pltpu.VMEM)
+    dma = pltpu.SemaphoreType.DMA
     return pl.pallas_call(
-        functools.partial(filter_kernel, count),
+        functools.partial(filter_kernel, count, groups),
         out_shape=(
             jax.ShapeDtypeStruct((states, owned), jnp.float32),
-            jax.ShapeDtypeStruct((states, owned), jnp.bfloat16),
-            jax.ShapeDtypeStruct((owned, states), jnp.bfloat16),
+            jax.ShapeDtypeStruct((rows, states), jnp.float32),
         ),
         in_specs=[vmem, vmem, vmem, pl.BlockSpec(memory_space=pltpu.SMEM)],
-        out_specs=(vmem, vmem, vmem),
+        out_specs=(vmem, vmem),
         scratch_shapes=[
             pltpu.VMEM((extent, depth), jnp.bfloat16),
             pltpu.VMEM((depth, states), jnp.bfloat16),
@@ -176,11 +347,25 @@
             pltpu.VMEM((extent, states), jnp.float32),
             pltpu.VMEM((both, states), jnp.float32),
             pltpu.VMEM((both, states), jnp.float32),
-            pltpu.VMEM((2, both, states), jnp.float32),
+            pltpu.VMEM((both, states), jnp.bfloat16),
+            pltpu.VMEM((2, both, states), jnp.bfloat16),
             pltpu.VMEM((shared, states), jnp.float32),
-            pltpu.SemaphoreType.DMA((2,)),
-            pltpu.SemaphoreType.DMA((2, 2)),
-            pltpu.SemaphoreType.DMA((2,)),
+            pltpu.VMEM((owned, states), jnp.bfloat16),
+            pltpu.VMEM((groups, states, owned), jnp.bfloat16),
+            pltpu.VMEM((groups, states, states), jnp.float32),
+            pltpu.VMEM((groups, pairs * rows, states), jnp.float32),
+            pltpu.VMEM((groups, pairs * rows, states), jnp.bfloat16),
+            pltpu.VMEM((chips, rows, states), jnp.bfloat16),
+            pltpu.VMEM((rows, states), jnp.float32),
+            dma((2,)),
+            dma((2, 2)),
+            dma((2,)),
+            dma((2, groups)),
+            dma((2, groups)),
+            dma((groups, pairs)),
+            dma((groups, pairs)),
+            dma((groups, pairs)),
+            dma((chips,)),
         ],
         compiler_params=pltpu.CompilerParams(
             collective_id=0, has_side_effects=True, vmem_limit_bytes=40 * 1024 * 1024
@@ -188,20 +373,12 @@
     )(start, links, cells, bounds)
 
 
-def per_device(start_block, connectivity, cell_matrices, bounds, count):
-    filtered, low, image = filtered_block(
-        start_block, connectivity, cell_matrices, bounds, count
-    )
-    all_low = lax.all_gather(low, "state", axis=0, tiled=True)
-    partial_value = matmul(all_low, image)
-    projected = lax.psum_scatter(partial_value, "cell", scatter_dimension=0, tiled=True)
-    return (filtered, projected)
-
-
 def solution(mesh):
     in_specs = (P("state", "cell"), P("cell", None), P("cell", None, None), P())
     out_specs = (P("state", "cell"), P("cell", "state"))
     return jax.shard_map(
-        functools.partial(per_device, count=mesh.shape["cell"]),
+        functools.partial(
+            filtered_block, count=mesh.shape["cell"], groups=mesh.shape["state"]
+        ),
         mesh=mesh, in_specs=in_specs, out_specs=out_specs, check_vma=False,
     )

time: 123 us -> 59.4 us (0.48)
  the two profiles are of different devices: /device:TPU:0 before, /device:TPU:7 now
where the time goes in v1:
time: 59.4 us; the launch traced here: 59.1 us
  Pallas kernels  55.7 us (94%)
  local copies, waits for them, and re-layouts  2.64 us (4%)
  between operations  0.68 us (1%)
    pallas_call x1, Pallas kernels, filtered_block(): pl.pallas_call(functools.partial(filter_kernel, count, groups), out_shape...  55.7 us
    unnamed x9, local copies, waits for them, and re-layouts  2.64 us

profile of v1, /device:TPU:7, one launch (start us, length us, event | category | flops | bytes accessed | tf_op | source)
XLA Modules:
  0.0 59.1 jit_solution(9701560395933061115)
XLA Ops:
  0.6 0.0 copy-start.2
  0.6 0.0 copy-start.1
  0.7 0.0 copy-start
  0.7 1.2 %copy.6.cells = bf16[2,343,343]{2,1,0:T(8,128)(2,1)S(1)} copy(bf16[2,343,343]{2,0,1:T(2,128)(2,1)} %param.6) | data formatting | bytes 941192 | tf_op args[2]
  1.8 0.0 copy-done.2
  1.8 0.0 copy-done.1
  1.9 0.0 copy-done
  1.9 55.7 %shard_map.59 = (f32[256,512]{1,0:T(8,128)S(1)}, f32[128,256]{1,0:T(8,128)S(1)}) custom-call(f32[256,512]{1,0:T(8,128)S(1)} %copy-done, s32[2,343]{1,0:T(2,128)S(1)} %copy-done.1, bf16[2,343,343]{2,1,0:T(8,128)(2,1)S(1)} %copy.6.cells, f32[3]{0:T(128)S(1)} %copy-done.2), custom_call_target="tpu_custom_call" | custom-call | tf_op jit(solution)/shard_map/pallas_call | solution.py:335
  57.6 0.8 %copy.9 = f32[256,512]{1,0:T(8,128)} copy(f32[256,512]{1,0:T(8,128)S(1)} %get-tuple-element.4) | data formatting | bytes 1048576
  58.4 0.7 %copy.10 = f32[128,256]{1,0:T(8,128)} copy(f32[128,256]{1,0:T(8,128)S(1)} %get-tuple-element.5) | data formatting | bytes 262144
Async XLA Ops:
  0.6 1.2 %copy-start.2 = (f32[3]{0:T(128)S(1)}, f32[3]{0:T(128)}, u32[]{:S(2)}) copy-start(f32[3]{0:T(128)} %bounds.1) | copy-start | bytes 40
  0.6 1.2 %copy-start.1 = (s32[2,343]{1,0:T(2,128)S(1)}, s32[2,343]{1,0:T(2,128)}, u32[]{:S(2)}) copy-start(s32[2,343]{1,0:T(2,128)} %links.1) | copy-start | bytes 8236
  0.7 1.2 %copy-start = (f32[256,512]{1,0:T(8,128)S(1)}, f32[256,512]{1,0:T(8,128)}, u32[]{:S(2)}) copy-start(f32[256,512]{1,0:T(8,128)} %start.1) | copy-start | bytes 1572868

commit v2 on v1

--- a/solution.py
+++ b/solution.py
@@ -175,17 +175,25 @@
     filtered[...] = result
     lows[place] = result.astype(jnp.bfloat16)
 
-    def hand_on(way, hop):
-        step = 1 - 2 * way
-        block = lax.rem(place - step * hop + groups, groups)
+    def piece_copy(way, hop, piece, block):
+        spot = lows.at[block, pl.ds(piece * rows, rows)]
         return pltpu.make_async_remote_copy(
-            src_ref=lows.at[block],
-            dst_ref=lows.at[block],
-            send_sem=along_send.at[way, hop],
-            recv_sem=along_recv.at[way, hop],
-            device_id={"state": lax.rem(place + step + groups, groups)},
-            device_id_type=MESH,
-        )
+            src_ref=spot,
+            dst_ref=spot,
+            send_sem=along_send.at[way, hop, piece],
+            recv_sem=along_recv.at[way, hop, piece],
+            device_id={"state": lax.rem(place + 1 - 2 * way + groups, groups)},
+            device_id_type=MESH,
+        )
+
+    def block_at(way, hop):
+        return lax.rem(place - (1 - 2 * way) * hop + groups, groups)
+
+    def hand_on(way, hop, piece):
+        return piece_copy(way, hop, piece, block_at(way, hop))
+
+    def arrival(way, hop, piece):
+        return piece_copy(way, hop, piece, block_at(way, hop + 1))
 
     def sends_at(way, hop):
         if way == 0:
@@ -197,26 +205,12 @@
             return place >= hop + 1
         return place + hop + 1 < groups
 
-    def block_at(way, hop):
-        return lax.rem(place - (1 - 2 * way) * (hop + 1) + groups, groups)
-
-    def arrival(way, hop):
-        step = 1 - 2 * way
-        block = block_at(way, hop)
-        return pltpu.make_async_remote_copy(
-            src_ref=lows.at[block],
-            dst_ref=lows.at[block],
-            send_sem=along_send.at[way, hop],
-            recv_sem=along_recv.at[way, hop],
-            device_id={"state": lax.rem(place + step + groups, groups)},
-            device_id_type=MESH,
-        )
-
     for way in range(2):
 
         @pl.when(sends_at(way, 0))
         def _():
-            hand_on(way, 0).start()
+            for piece in range(owners):
+                hand_on(way, 0, piece).start()
 
     image[shared:, :] = matmul(matrix[both:, :], stack[...]).astype(jnp.bfloat16)
     last = DEGREE % 2
@@ -224,84 +218,98 @@
         copy.wait()
     image[0:shared, :] = (outgoing[0:shared, :] + incoming[last, 0:shared, :]).astype(jnp.bfloat16)
 
-    def swap(block, pair):
+    def swap(block, piece):
         return pltpu.make_async_remote_copy(
-            src_ref=parts.at[block, pl.ds((2 * pair + 1 - core) * rows, rows)],
-            dst_ref=swapped.at[block, pl.ds(pair * rows, rows)],
-            send_sem=swap_send.at[block, pair],
-            recv_sem=swap_recv.at[block, pair],
+            src_ref=parts.at[block, pl.ds(piece * rows, rows)],
+            dst_ref=swapped.at[block, pl.ds(piece // 2 * rows, rows)],
+            send_sem=swap_send.at[block, piece // 2],
+            recv_sem=swap_recv.at[block, piece // 2],
             device_id={"cell": chip * 2 + 1 - core},
             device_id_type=MESH,
         )
 
-    def owner_of(block, pair):
-        return block * (owners // 2) + pair
-
-    def shipping(block, pair):
+    def owner_of(block, piece):
+        return block * (owners // 2) + piece // 2
+
+    def shipping(block, piece):
         return pltpu.make_async_remote_copy(
-            src_ref=ship.at[block, pl.ds(pair * rows, rows)],
+            src_ref=ship.at[block, pl.ds(piece // 2 * rows, rows)],
             dst_ref=gathered.at[chip],
-            send_sem=ship_send.at[block, pair],
+            send_sem=ship_send.at[block, piece // 2],
             recv_sem=ship_recv.at[chip],
-            device_id={"cell": 2 * owner_of(block, pair) + core},
-            device_id_type=MESH,
-        )
-
-    def multiply(block):
-        parts[block] = matmul(lows[block], image[...])
-        for pair in range(owners // 2):
-            swap(block, pair).start()
-
-    def pass_to_owners(block):
-        for pair in range(owners // 2):
-            swap(block, pair).wait()
-            kept = pl.ds(pl.multiple_of((2 * pair + core) * rows, rows), rows)
-            total = parts[block, kept, :] + swapped[block, pair * rows : (pair + 1) * rows, :]
-
-            @pl.when(owner_of(block, pair) == chip)
+            device_id={"cell": 2 * owner_of(block, piece) + core},
+            device_id_type=MESH,
+        )
+
+    def multiply(block, piece):
+        here = slice(piece * rows, (piece + 1) * rows)
+        parts[block, here, :] = matmul(lows[block, here, :], image[...])
+
+        @pl.when(core != piece % 2)
+        def _():
+            swap(block, piece).start()
+
+    def pass_to_owner(block, piece):
+        here = slice(piece * rows, (piece + 1) * rows)
+        there = slice(piece // 2 * rows, (piece // 2 + 1) * rows)
+
+        @pl.when(core == piece % 2)
+        def _():
+            swap(block, piece).wait_recv()
+            total = parts[block, here, :] + swapped[block, there, :]
+
+            @pl.when(owner_of(block, piece) == chip)
             def _():
                 mine[...] = total
 
-            @pl.when(owner_of(block, pair) != chip)
-            def _():
-                ship[block, pair * rows : (pair + 1) * rows, :] = total.astype(jnp.bfloat16)
-                shipping(block, pair).start()
-
-    multiply(place)
-    pass_to_owners(place)
+            @pl.when(owner_of(block, piece) != chip)
+            def _():
+                ship[block, there, :] = total
+                shipping(block, piece).start()
+
+    for piece in range(owners):
+        multiply(place, piece)
+    for piece in range(owners):
+        pass_to_owner(place, piece)
     for hop in range(groups - 1):
-        for way in range(2):
-
-            @pl.when(receives_at(way, hop))
-            def _():
-                arrival(way, hop).wait_recv()
-                if hop + 1 < groups - 1:
-
-                    @pl.when(sends_at(way, hop + 1))
-                    def _():
-                        hand_on(way, hop + 1).start()
-
-                multiply(block_at(way, hop))
-
-        for way in range(2):
-
-            @pl.when(receives_at(way, hop))
-            def _():
-                pass_to_owners(block_at(way, hop))
+        for piece in range(owners):
+            for way in range(2):
+
+                @pl.when(receives_at(way, hop))
+                def _():
+                    arrival(way, hop, piece).wait_recv()
+                    if hop + 1 < groups - 1:
+
+                        @pl.when(sends_at(way, hop + 1))
+                        def _():
+                            hand_on(way, hop + 1, piece).start()
+
+                    multiply(block_at(way, hop + 1), piece)
+
+            for way in range(2):
+
+                @pl.when(receives_at(way, hop))
+                def _():
+                    pass_to_owner(block_at(way, hop + 1), piece)
 
     for way in range(2):
         for hop in range(groups - 1):
 
             @pl.when(sends_at(way, hop))
             def _():
-                hand_on(way, hop).wait_send()
+                for piece in range(owners):
+                    hand_on(way, hop, piece).wait_send()
 
     for block in range(groups):
-        for pair in range(owners // 2):
-
-            @pl.when(owner_of(block, pair) != chip)
-            def _():
-                shipping(block, pair).wait_send()
+        for piece in range(owners):
+
+            @pl.when(core != piece % 2)
+            def _():
+                swap(block, piece).wait_send()
+
+            @pl.when(jnp.logical_and(core == piece % 2, owner_of(block, piece) != chip))
+            def _():
+                shipping(block, piece).wait_send()
 
     for other in range(chips):
 
@@ -315,7 +323,7 @@
                 device_id={"cell": 2 * other + core},
                 device_id_type=MESH,
             ).wait_recv()
-            mine[...] += gathered[other].astype(jnp.float32)
+            mine[...] += gathered[other]
 
     projected[...] = mine[...]
 
@@ -354,14 +362,14 @@
             pltpu.VMEM((groups, states, owned), jnp.bfloat16),
             pltpu.VMEM((groups, states, states), jnp.float32),
             pltpu.VMEM((groups, pairs * rows, states), jnp.float32),
-            pltpu.VMEM((groups, pairs * rows, states), jnp.bfloat16),
-            pltpu.VMEM((chips, rows, states), jnp.bfloat16),
+            pltpu.VMEM((groups, pairs * rows, states), jnp.float32),
+            pltpu.VMEM((chips, rows, states), jnp.float32),
             pltpu.VMEM((rows, states), jnp.float32),
             dma((2,)),
             dma((2, 2)),
             dma((2,)),
-            dma((2, groups)),
-            dma((2, groups)),
+            dma((2, groups, 2 * pairs)),
+            dma((2, groups, 2 * pairs)),
             dma((groups, pairs)),
             dma((groups, pairs)),
             dma((groups, pairs)),

time: 59.4 us -> 58.9 us (level)
  no operation moved by 1% of the time
where the time goes in v2:
time: 58.9 us; the launch traced here: 58.7 us
  Pallas kernels  55.4 us (94%)
  local copies, waits for them, and re-layouts  2.64 us (4%)
  between operations  0.68 us (1%)
    pallas_call x1, Pallas kernels, filtered_block(): pl.pallas_call(functools.partial(filter_kernel, count, groups), out_shape...  55.4 us
    unnamed x9, local copies, waits for them, and re-layouts  2.64 us

profile of v2, /device:TPU:7, one launch (start us, length us, event | category | flops | bytes accessed | tf_op | source)
XLA Modules:
  0.0 58.7 jit_solution(12615843350721858087)
XLA Ops:
  0.6 0.0 copy-start.2
  0.6 0.0 copy-start.1
  0.7 0.0 copy-start
  0.7 1.2 %copy.6.cells = bf16[2,343,343]{2,1,0:T(8,128)(2,1)S(1)} copy(bf16[2,343,343]{2,0,1:T(2,128)(2,1)} %param.6) | data formatting | bytes 941192 | tf_op args[2]
  1.8 0.0 copy-done.2
  1.8 0.0 copy-done.1
  1.9 0.0 copy-done
  1.9 55.4 %shard_map.59 = (f32[256,512]{1,0:T(8,128)S(1)}, f32[128,256]{1,0:T(8,128)S(1)}) custom-call(f32[256,512]{1,0:T(8,128)S(1)} %copy-done, s32[2,343]{1,0:T(2,128)S(1)} %copy-done.1, bf16[2,343,343]{2,1,0:T(8,128)(2,1)S(1)} %copy.6.cells, f32[3]{0:T(128)S(1)} %copy-done.2), custom_call_target="tpu_custom_call" | custom-call | tf_op jit(solution)/shard_map/pallas_call | solution.py:343
  57.3 0.8 %copy.9 = f32[256,512]{1,0:T(8,128)} copy(f32[256,512]{1,0:T(8,128)S(1)} %get-tuple-element.4) | data formatting | bytes 1048576
  58.1 0.7 %copy.10 = f32[128,256]{1,0:T(8,128)} copy(f32[128,256]{1,0:T(8,128)S(1)} %get-tuple-element.5) | data formatting | bytes 262144
Async XLA Ops:
  0.6 1.2 %copy-start.2 = (f32[3]{0:T(128)S(1)}, f32[3]{0:T(128)}, u32[]{:S(2)}) copy-start(f32[3]{0:T(128)} %bounds.1) | copy-start | bytes 40
  0.6 1.2 %copy-start.1 = (s32[2,343]{1,0:T(2,128)S(1)}, s32[2,343]{1,0:T(2,128)}, u32[]{:S(2)}) copy-start(s32[2,343]{1,0:T(2,128)} %links.1) | copy-start | bytes 8236
  0.7 1.2 %copy-start = (f32[256,512]{1,0:T(8,128)S(1)}, f32[256,512]{1,0:T(8,128)}, u32[]{:S(2)}) copy-start(f32[256,512]{1,0:T(8,128)} %start.1) | copy-start | bytes 1572868

commit v3 on v2

--- a/solution.py
+++ b/solution.py
@@ -18,7 +18,7 @@
 def filter_kernel(
     count, groups, start, links, cells, bounds, filtered, projected,
     matrix, stack, field, before, inner, outgoing, rounded_out, incoming, ghost,
-    image, lows, parts, swapped, ship, gathered, mine,
+    image, lows, low_ends, parts, swapped, ship, gathered, mine,
     sends, receives, ghost_sems, along_send, along_recv, swap_send, swap_recv,
     ship_send, ship_recv,
 ):
@@ -145,15 +145,15 @@
     sigma_first = half / (lowest - centre)
     tau = 2.0 / sigma_first
 
-    def degree_step(step, carry):
-        alpha, beta, sigma = carry
-        slot = lax.rem(step, 2)
+    def step_rest(alpha, beta):
         new_rest = (
             matmul(matrix[both:, :], stack[...]) - centre * field[both:, :]
         ) * alpha - beta * before[both:, :]
         before[both:, :] = field[both:, :]
         field[both:, :] = new_rest
-        put_rest()
+
+    def step_shared(step, alpha, beta):
+        slot = lax.rem(step, 2)
         for copy in copies(slot):
             copy.wait()
         new_shared = (
@@ -164,24 +164,26 @@
         put_shared()
         for copy in copies(lax.rem(step + 1, 2)):
             copy.start()
+
+    def degree_step(step, carry):
+        alpha, beta, sigma = carry
+        step_rest(alpha, beta)
+        put_rest()
+        step_shared(step, alpha, beta)
         sigma_new = 1.0 / (tau - sigma)
         return 2.0 * sigma_new / half, sigma * sigma_new, sigma_new
 
-    lax.fori_loop(
-        0, DEGREE, degree_step, (sigma_first / half, jnp.zeros_like(half), sigma_first)
+    alpha, beta, _ = lax.fori_loop(
+        0, DEGREE - 1, degree_step, (sigma_first / half, jnp.zeros_like(half), sigma_first)
     )
 
-    result = jnp.concatenate([field[0:shared, :], field[both:, :]], axis=0).T
-    filtered[...] = result
-    lows[place] = result.astype(jnp.bfloat16)
-
-    def piece_copy(way, hop, piece, block):
-        spot = lows.at[block, pl.ds(piece * rows, rows)]
+    def piece_copy(way, hop, piece, block, part):
+        spot = (lows, low_ends)[part].at[block, pl.ds(piece * rows, rows)]
         return pltpu.make_async_remote_copy(
             src_ref=spot,
             dst_ref=spot,
-            send_sem=along_send.at[way, hop, piece],
-            recv_sem=along_recv.at[way, hop, piece],
+            send_sem=along_send.at[way, hop, piece, part],
+            recv_sem=along_recv.at[way, hop, piece, part],
             device_id={"state": lax.rem(place + 1 - 2 * way + groups, groups)},
             device_id_type=MESH,
         )
@@ -189,11 +191,11 @@
     def block_at(way, hop):
         return lax.rem(place - (1 - 2 * way) * hop + groups, groups)
 
-    def hand_on(way, hop, piece):
-        return piece_copy(way, hop, piece, block_at(way, hop))
-
-    def arrival(way, hop, piece):
-        return piece_copy(way, hop, piece, block_at(way, hop + 1))
+    def hand_on(way, hop, piece, part):
+        return piece_copy(way, hop, piece, block_at(way, hop), part)
+
+    def arrival(way, hop, piece, part):
+        return piece_copy(way, hop, piece, block_at(way, hop + 1), part)
 
     def sends_at(way, hop):
         if way == 0:
@@ -205,18 +207,29 @@
             return place >= hop + 1
         return place + hop + 1 < groups
 
-    for way in range(2):
-
-        @pl.when(sends_at(way, 0))
-        def _():
-            for piece in range(owners):
-                hand_on(way, 0, piece).start()
-
-    image[shared:, :] = matmul(matrix[both:, :], stack[...]).astype(jnp.bfloat16)
+    def send_own(part):
+        for way in range(2):
+
+            @pl.when(sends_at(way, 0))
+            def _():
+                for piece in range(owners):
+                    hand_on(way, 0, piece, part).start()
+
+    early = owned - 128
+    step_rest(alpha, beta)
+    lows[place] = field[both : both + early, :].T.astype(jnp.bfloat16)
+    send_own(0)
+    put_rest()
+    step_shared(DEGREE - 1, alpha, beta)
+    tail = jnp.concatenate([field[both + early :, :], field[0:shared, :]], axis=0)
+    low_ends[place] = tail.T.astype(jnp.bfloat16)
+    send_own(1)
+    image[0:rest, :] = matmul(matrix[both:, :], stack[...]).astype(jnp.bfloat16)
+    filtered[...] = jnp.concatenate([field[0:shared, :], field[both:, :]], axis=0).T
     last = DEGREE % 2
     for copy in copies(last):
         copy.wait()
-    image[0:shared, :] = (outgoing[0:shared, :] + incoming[last, 0:shared, :]).astype(jnp.bfloat16)
+    image[rest:, :] = (outgoing[0:shared, :] + incoming[last, 0:shared, :]).astype(jnp.bfloat16)
 
     def swap(block, piece):
         return pltpu.make_async_remote_copy(
@@ -243,7 +256,9 @@
 
     def multiply(block, piece):
         here = slice(piece * rows, (piece + 1) * rows)
-        parts[block, here, :] = matmul(lows[block, here, :], image[...])
+        parts[block, here, :] = matmul(lows[block, here, :], image[0:early, :]) + matmul(
+            low_ends[block, here, :], image[early:, :]
+        )
 
         @pl.when(core != piece % 2)
         def _():
@@ -277,12 +292,13 @@
 
                 @pl.when(receives_at(way, hop))
                 def _():
-                    arrival(way, hop, piece).wait_recv()
-                    if hop + 1 < groups - 1:
-
-                        @pl.when(sends_at(way, hop + 1))
-                        def _():
-                            hand_on(way, hop + 1, piece).start()
+                    for part in range(2):
+                        arrival(way, hop, piece, part).wait_recv()
+                        if hop + 1 < groups - 1:
+
+                            @pl.when(sends_at(way, hop + 1))
+                            def _():
+                                hand_on(way, hop + 1, piece, part).start()
 
                     multiply(block_at(way, hop + 1), piece)
 
@@ -298,7 +314,8 @@
             @pl.when(sends_at(way, hop))
             def _():
                 for piece in range(owners):
-                    hand_on(way, hop, piece).wait_send()
+                    for part in range(2):
+                        hand_on(way, hop, piece, part).wait_send()
 
     for block in range(groups):
         for piece in range(owners):
@@ -359,7 +376,8 @@
             pltpu.VMEM((2, both, states), jnp.bfloat16),
             pltpu.VMEM((shared, states), jnp.float32),
             pltpu.VMEM((owned, states), jnp.bfloat16),
-            pltpu.VMEM((groups, states, owned), jnp.bfloat16),
+            pltpu.VMEM((groups, states, owned - 128), jnp.bfloat16),
+            pltpu.VMEM((groups, states, 128), jnp.bfloat16),
             pltpu.VMEM((groups, states, states), jnp.float32),
             pltpu.VMEM((groups, pairs * rows, states), jnp.float32),
             pltpu.VMEM((groups, pairs * rows, states), jnp.float32),
@@ -368,8 +386,8 @@
             dma((2,)),
             dma((2, 2)),
             dma((2,)),
-            dma((2, groups, 2 * pairs)),
-            dma((2, groups, 2 * pairs)),
+            dma((2, groups, 2 * pairs, 2)),
+            dma((2, groups, 2 * pairs, 2)),
             dma((groups, pairs)),
             dma((groups, pairs)),
             dma((groups, pairs)),

time: 58.9 us -> 58.5 us (level)
  no operation moved by 1% of the time
where the time goes in v3:
time: 58.5 us; the launch traced here: 58.3 us
  Pallas kernels  55 us (94%)
  local copies, waits for them, and re-layouts  2.64 us (5%)
  between operations  0.68 us (1%)
    pallas_call x1, Pallas kernels, filtered_block(): pl.pallas_call(functools.partial(filter_kernel, count, groups), out_shape...  55 us
    unnamed x9, local copies, waits for them, and re-layouts  2.64 us

profile of v3, /device:TPU:7, one launch (start us, length us, event | category | flops | bytes accessed | tf_op | source)
XLA Modules:
  0.0 58.3 jit_solution(378399195650418533)
XLA Ops:
  0.6 0.0 copy-start.2
  0.6 0.0 copy-start.1
  0.7 0.0 copy-start
  0.7 1.2 %copy.6.cells = bf16[2,343,343]{2,1,0:T(8,128)(2,1)S(1)} copy(bf16[2,343,343]{2,0,1:T(2,128)(2,1)} %param.6) | data formatting | bytes 941192 | tf_op args[2]
  1.8 0.0 copy-done.2
  1.8 0.0 copy-done.1
  1.9 0.0 copy-done
  1.9 55.0 %shard_map.59 = (f32[256,512]{1,0:T(8,128)S(1)}, f32[128,256]{1,0:T(8,128)S(1)}) custom-call(f32[256,512]{1,0:T(8,128)S(1)} %copy-done, s32[2,343]{1,0:T(2,128)S(1)} %copy-done.1, bf16[2,343,343]{2,1,0:T(8,128)(2,1)S(1)} %copy.6.cells, f32[3]{0:T(128)S(1)} %copy-done.2), custom_call_target="tpu_custom_call" | custom-call | tf_op jit(solution)/shard_map/pallas_call | solution.py:360
  56.9 0.8 %copy.9 = f32[256,512]{1,0:T(8,128)} copy(f32[256,512]{1,0:T(8,128)S(1)} %get-tuple-element.4) | data formatting | bytes 1048576
  57.7 0.7 %copy.10 = f32[128,256]{1,0:T(8,128)} copy(f32[128,256]{1,0:T(8,128)S(1)} %get-tuple-element.5) | data formatting | bytes 262144
Async XLA Ops:
  0.6 1.2 %copy-start.2 = (f32[3]{0:T(128)S(1)}, f32[3]{0:T(128)}, u32[]{:S(2)}) copy-start(f32[3]{0:T(128)} %bounds.1) | copy-start | bytes 40
  0.6 1.2 %copy-start.1 = (s32[2,343]{1,0:T(2,128)S(1)}, s32[2,343]{1,0:T(2,128)}, u32[]{:S(2)}) copy-start(s32[2,343]{1,0:T(2,128)} %links.1) | copy-start | bytes 8236
  0.7 1.2 %copy-start = (f32[256,512]{1,0:T(8,128)S(1)}, f32[256,512]{1,0:T(8,128)}, u32[]{:S(2)}) copy-start(f32[256,512]{1,0:T(8,128)} %start.1) | copy-start | bytes 1572868

commit v4 on v3

--- a/solution.py
+++ b/solution.py
@@ -282,10 +282,20 @@
                 ship[block, there, :] = total
                 shipping(block, piece).start()
 
+    def pass_own():
+        for piece in range(owners):
+            pass_to_owner(place, piece)
+
+    def pass_arrived(hop, piece):
+        for way in range(2):
+
+            @pl.when(receives_at(way, hop))
+            def _():
+                pass_to_owner(block_at(way, hop + 1), piece)
+
     for piece in range(owners):
         multiply(place, piece)
-    for piece in range(owners):
-        pass_to_owner(place, piece)
+    waiting = [pass_own]
     for hop in range(groups - 1):
         for piece in range(owners):
             for way in range(2):
@@ -302,11 +312,13 @@
 
                     multiply(block_at(way, hop + 1), piece)
 
-            for way in range(2):
-
-                @pl.when(receives_at(way, hop))
-                def _():
-                    pass_to_owner(block_at(way, hop + 1), piece)
+            for pending in waiting:
+                pending()
+            waiting = [functools.partial(pass_arrived, hop, piece)]
+            if hop == groups - 2:
+                waiting.pop()()
+    for pending in waiting:
+        pending()
 
     for way in range(2):
         for hop in range(groups - 1):

time: 58.5 us -> 57.9 us (0.990)
  Pallas kernels: 55 us -> 54.4 us
where the time goes in v4:
time: 57.9 us; the launch traced here: 57.8 us
  Pallas kernels  54.4 us (94%)
  local copies, waits for them, and re-layouts  2.64 us (5%)
  between operations  0.68 us (1%)
    pallas_call x1, Pallas kernels, filtered_block(): pl.pallas_call(functools.partial(filter_kernel, count, groups), out_shape...  54.4 us
    unnamed x9, local copies, waits for them, and re-layouts  2.64 us

profile of v4, /device:TPU:7, one launch (start us, length us, event | category | flops | bytes accessed | tf_op | source)
XLA Modules:
  0.0 57.8 jit_solution(6021886969222541142)
XLA Ops:
  0.6 0.0 copy-start.2
  0.6 0.0 copy-start.1
  0.7 0.0 copy-start
  0.7 1.2 %copy.6.cells = bf16[2,343,343]{2,1,0:T(8,128)(2,1)S(1)} copy(bf16[2,343,343]{2,0,1:T(2,128)(2,1)} %param.6) | data formatting | bytes 941192 | tf_op args[2]
  1.8 0.0 copy-done.2
  1.8 0.0 copy-done.1
  1.9 0.0 copy-done
  1.9 54.4 %shard_map.59 = (f32[256,512]{1,0:T(8,128)S(1)}, f32[128,256]{1,0:T(8,128)S(1)}) custom-call(f32[256,512]{1,0:T(8,128)S(1)} %copy-done, s32[2,343]{1,0:T(2,128)S(1)} %copy-done.1, bf16[2,343,343]{2,1,0:T(8,128)(2,1)S(1)} %copy.6.cells, f32[3]{0:T(128)S(1)} %copy-done.2), custom_call_target="tpu_custom_call" | custom-call | tf_op jit(solution)/shard_map/pallas_call | solution.py:372
  56.3 0.8 %copy.9 = f32[256,512]{1,0:T(8,128)} copy(f32[256,512]{1,0:T(8,128)S(1)} %get-tuple-element.4) | data formatting | bytes 1048576
  57.1 0.7 %copy.10 = f32[128,256]{1,0:T(8,128)} copy(f32[128,256]{1,0:T(8,128)S(1)} %get-tuple-element.5) | data formatting | bytes 262144
Async XLA Ops:
  0.6 1.2 %copy-start.2 = (f32[3]{0:T(128)S(1)}, f32[3]{0:T(128)}, u32[]{:S(2)}) copy-start(f32[3]{0:T(128)} %bounds.1) | copy-start | bytes 40
  0.6 1.2 %copy-start.1 = (s32[2,343]{1,0:T(2,128)S(1)}, s32[2,343]{1,0:T(2,128)}, u32[]{:S(2)}) copy-start(s32[2,343]{1,0:T(2,128)} %links.1) | copy-start | bytes 8236
  0.7 1.2 %copy-start = (f32[256,512]{1,0:T(8,128)S(1)}, f32[256,512]{1,0:T(8,128)}, u32[]{:S(2)}) copy-start(f32[256,512]{1,0:T(8,128)} %start.1) | copy-start | bytes 1572868

commit v5 on v4

--- a/solution.py
+++ b/solution.py
@@ -61,8 +61,6 @@
 
     field[0:both, :] = start[:, 0:both].T
     stack[0:both, :] = field[0:both, :].astype(jnp.bfloat16)
-    beside = jnp.minimum(place, 1) + jnp.minimum(groups - 1 - place, 1)
-    pl.semaphore_wait(barrier, 1 + chips + beside)
     ghost_copy = pltpu.make_async_remote_copy(
         src_ref=outgoing.at[pl.ds(0, shared)],
         dst_ref=ghost,
@@ -72,7 +70,6 @@
         device_id_type=MESH,
     )
     outgoing[0:shared, :] = field[0:shared, :]
-    ghost_copy.start()
 
     whole = start[...].T
     field[both:, :] = whole[shared:, :]
@@ -92,6 +89,10 @@
         matrix[:, cell * both : (cell + 1) * both] = placed[:, 0:both]
         begin = first if cell == 0 else second
         matrix[:, begin : begin + rest] = placed[:, both:]
+        if cell == 0:
+            beside = jnp.minimum(place, 1) + jnp.minimum(groups - 1 - place, 1)
+            pl.semaphore_wait(barrier, 1 + chips + beside)
+            ghost_copy.start()
     if second > first + rest:
         matrix[:, first + rest : second] = jnp.zeros((extent, second - first - rest), jnp.bfloat16)
         stack[first + rest : second, :] = jnp.zeros((second - first - rest, states), jnp.bfloat16)

time: 57.9 us -> 57.9 us (level)
  no operation moved by 1% of the time
where the time goes in v5:
time: 57.9 us; the launch traced here: 57.8 us
  Pallas kernels  54.4 us (94%)
  local copies, waits for them, and re-layouts  2.64 us (5%)
  between operations  0.68 us (1%)
    pallas_call x1, Pallas kernels, filtered_block(): pl.pallas_call(functools.partial(filter_kernel, count, groups), out_shape...  54.4 us
    unnamed x9, local copies, waits for them, and re-layouts  2.64 us

profile of v5, /device:TPU:7, one launch (start us, length us, event | category | flops | bytes accessed | tf_op | source)
XLA Modules:
  0.0 57.8 jit_solution(18416169414391261840)
XLA Ops:
  0.6 0.0 copy-start.2
  0.6 0.0 copy-start.1
  0.7 0.0 copy-start
  0.7 1.2 %copy.6.cells = bf16[2,343,343]{2,1,0:T(8,128)(2,1)S(1)} copy(bf16[2,343,343]{2,0,1:T(2,128)(2,1)} %param.6) | data formatting | bytes 941192 | tf_op args[2]
  1.8 0.0 copy-done.2
  1.8 0.0 copy-done.1
  1.9 0.0 copy-done
  1.9 54.4 %shard_map.59 = (f32[256,512]{1,0:T(8,128)S(1)}, f32[128,256]{1,0:T(8,128)S(1)}) custom-call(f32[256,512]{1,0:T(8,128)S(1)} %copy-done, s32[2,343]{1,0:T(2,128)S(1)} %copy-done.1, bf16[2,343,343]{2,1,0:T(8,128)(2,1)S(1)} %copy.6.cells, f32[3]{0:T(128)S(1)} %copy-done.2), custom_call_target="tpu_custom_call" | custom-call | tf_op jit(solution)/shard_map/pallas_call | solution.py:373
  56.3 0.8 %copy.9 = f32[256,512]{1,0:T(8,128)} copy(f32[256,512]{1,0:T(8,128)S(1)} %get-tuple-element.4) | data formatting | bytes 1048576
  57.1 0.7 %copy.10 = f32[128,256]{1,0:T(8,128)} copy(f32[128,256]{1,0:T(8,128)S(1)} %get-tuple-element.5) | data formatting | bytes 262144
Async XLA Ops:
  0.6 1.2 %copy-start.2 = (f32[3]{0:T(128)S(1)}, f32[3]{0:T(128)}, u32[]{:S(2)}) copy-start(f32[3]{0:T(128)} %bounds.1) | copy-start | bytes 40
  0.6 1.2 %copy-start.1 = (s32[2,343]{1,0:T(2,128)S(1)}, s32[2,343]{1,0:T(2,128)}, u32[]{:S(2)}) copy-start(s32[2,343]{1,0:T(2,128)} %links.1) | copy-start | bytes 8236
  0.7 1.2 %copy-start = (f32[256,512]{1,0:T(8,128)S(1)}, f32[256,512]{1,0:T(8,128)}, u32[]{:S(2)}) copy-start(f32[256,512]{1,0:T(8,128)} %start.1) | copy-start | bytes 1572868

commit v6 on v5

--- a/solution.py
+++ b/solution.py
@@ -155,13 +155,13 @@
 
     def step_shared(step, alpha, beta):
         slot = lax.rem(step, 2)
+        known = (
+            outgoing[...] - centre * field[0:both, :]
+        ) * alpha - beta * before[0:both, :]
+        before[0:both, :] = field[0:both, :]
         for copy in copies(slot):
             copy.wait()
-        new_shared = (
-            outgoing[...] + incoming[slot] - centre * field[0:both, :]
-        ) * alpha - beta * before[0:both, :]
-        before[0:both, :] = field[0:both, :]
-        field[0:both, :] = new_shared
+        field[0:both, :] = known + alpha * incoming[slot]
         put_shared()
         for copy in copies(lax.rem(step + 1, 2)):
             copy.start()

time: 57.9 us -> 57.8 us (level)
  no operation moved by 1% of the time
where the time goes in v6:
time: 57.8 us; the launch traced here: 57.6 us
  Pallas kernels  54.3 us (94%)
  local copies, waits for them, and re-layouts  2.64 us (5%)
  between operations  0.68 us (1%)
    pallas_call x1, Pallas kernels, filtered_block(): pl.pallas_call(functools.partial(filter_kernel, count, groups), out_shape...  54.3 us
    unnamed x9, local copies, waits for them, and re-layouts  2.64 us

profile of v6, /device:TPU:7, one launch (start us, length us, event | category | flops | bytes accessed | tf_op | source)
XLA Modules:
  0.0 57.6 jit_solution(3719439192760054830)
XLA Ops:
  0.6 0.0 copy-start.2
  0.6 0.0 copy-start.1
  0.7 0.0 copy-start
  0.7 1.2 %copy.6.cells = bf16[2,343,343]{2,1,0:T(8,128)(2,1)S(1)} copy(bf16[2,343,343]{2,0,1:T(2,128)(2,1)} %param.6) | data formatting | bytes 941192 | tf_op args[2]
  1.8 0.0 copy-done.2
  1.8 0.0 copy-done.1
  1.9 0.0 copy-done
  1.9 54.3 %shard_map.59 = (f32[256,512]{1,0:T(8,128)S(1)}, f32[128,256]{1,0:T(8,128)S(1)}) custom-call(f32[256,512]{1,0:T(8,128)S(1)} %copy-done, s32[2,343]{1,0:T(2,128)S(1)} %copy-done.1, bf16[2,343,343]{2,1,0:T(8,128)(2,1)S(1)} %copy.6.cells, f32[3]{0:T(128)S(1)} %copy-done.2), custom_call_target="tpu_custom_call" | custom-call | tf_op jit(solution)/shard_map/pallas_call | solution.py:373
  56.2 0.8 %copy.9 = f32[256,512]{1,0:T(8,128)} copy(f32[256,512]{1,0:T(8,128)S(1)} %get-tuple-element.4) | data formatting | bytes 1048576
  57.0 0.7 %copy.10 = f32[128,256]{1,0:T(8,128)} copy(f32[128,256]{1,0:T(8,128)S(1)} %get-tuple-element.5) | data formatting | bytes 262144
Async XLA Ops:
  0.6 1.2 %copy-start.2 = (f32[3]{0:T(128)S(1)}, f32[3]{0:T(128)}, u32[]{:S(2)}) copy-start(f32[3]{0:T(128)} %bounds.1) | copy-start | bytes 40
  0.6 1.2 %copy-start.1 = (s32[2,343]{1,0:T(2,128)S(1)}, s32[2,343]{1,0:T(2,128)}, u32[]{:S(2)}) copy-start(s32[2,343]{1,0:T(2,128)} %links.1) | copy-start | bytes 8236
  0.7 1.2 %copy-start = (f32[256,512]{1,0:T(8,128)S(1)}, f32[256,512]{1,0:T(8,128)}, u32[]{:S(2)}) copy-start(f32[256,512]{1,0:T(8,128)} %start.1) | copy-start | bytes 1572868
